TPU v7x, 256 devices: a whole 4x4x8 slice. The times are simulated.
256 devices in a mesh: seq: 32 (over z, x), head: 8 (over y, core).
Axes of the slice: x: 4, y: 4, z: 8, core: 2. Of those that a mesh axis runs over, the one named last changes fastest.
Arguments:
- mixer_input: bfloat16 [65536, 5120], P('seq', 'head'), may hold values from -6 to 6
- write_rows: bfloat16 [65536, 128], P(('seq', 'head')), may hold values from -1.796875 to 1.796875
- read_rows: bfloat16 [65536, 128], P(('seq', 'head')), may hold values from -1.796875 to 1.796875
- log_decay: float32 [80, 65536], P('head', 'seq'), may hold values from -2 to 0, as said below
- skip_gain: float32 [80], P('head'), may hold values from 0.25 to 1.75
- reset_offsets: int32 [32, 4], P('seq'), may hold values from 0 to 2048, as said below
- grad_out: bfloat16 [65536, 5120], P('seq', 'head'), may hold values from -6 to 6
Outputs:
- grad_input: bfloat16 [65536, 5120], P('seq', 'head')
- grad_write: float32 [65536, 128], P(('seq', 'head'))
- grad_read: float32 [65536, 128], P(('seq', 'head'))
Inputs may be any that keep to these rules, and one draw needn't show every extreme that they name: `log_decay`: every entry is negative. `reset_offsets`: row d lists, in increasing order, the offsets within block d of 2048 tokens at which an episode begins; unused slots hold 2048 and stand after the used ones; some row uses all 4 slots.
All inputs are finite; a program needn't handle non-finite values.
Results may differ from a plain program's by a relative error of at most 0.0055.
Values may be sent and summed in bfloat16 or wider, within the bound.
No kernel may reach another device: no remote copies, remote signals or barrier semaphores. Data moves between devices by JAX's collectives and lax.ppermute only.
A program may use at most 192 MiB of HBM per device.

v0:
```python
import jax
import jax.numpy as jnp
from jax import lax
from jax.sharding import PartitionSpec as P

SPAN = 256


def entering(part, axis, combine, identity, reverse):
    count = lax.axis_size(axis)
    place = lax.axis_index(axis)
    ahead = count - 1 - place if reverse else place
    gathered = jax.tree.map(lambda a: lax.all_gather(a, axis), part)
    state = jax.tree.map(lambda a, e: jnp.zeros_like(a) + jnp.asarray(e, a.dtype), part, identity)

    def one(step, state):
        source = count - 1 - step if reverse else step
        return combine(
            state, jax.tree.map(lambda a: lax.dynamic_index_in_dim(a, source, 0, False), gathered)
        )

    return lax.fori_loop(0, ahead, one, state)


def span_update(carry_state, inputs, skip_gain):
    feature_part, write_part, read_part, log_part, reset_part = inputs
    span_len = reset_part.shape[0]
    cum_log = jnp.cumsum(log_part, axis=1)
    reset_count = jnp.cumsum(reset_part)
    input_gain = jnp.sqrt(-jnp.expm1(2.0 * log_part))
    positions = jnp.arange(span_len)
    allowed = (positions[:, None] >= positions[None, :]) & (
        reset_count[:, None] == reset_count[None, :]
    )
    spread = cum_log[:, :, None] - cum_log[:, None, :]
    decay_matrix = jnp.exp(jnp.where(allowed[None], spread, -1e30))
    scores = jnp.dot(read_part, write_part.T, precision=lax.Precision.HIGHEST)
    weights = decay_matrix * scores[None] * input_gain[:, None, :]
    result = jnp.einsum("hts,shp->thp", weights, feature_part, precision=lax.Precision.HIGHEST)
    entry_decay = jnp.exp(cum_log) * (reset_count == 0)[None, :]
    carried = jnp.einsum("tn,hnp->thp", read_part, carry_state, precision=lax.Precision.HIGHEST)
    result = result + carried * entry_decay.T[:, :, None] + skip_gain[None, :, None] * feature_part
    tail_weight = (
        jnp.exp(cum_log[:, -1:] - cum_log) * (reset_count == reset_count[-1])[None, :] * input_gain
    )
    block_decay = jnp.exp(cum_log[:, -1]) * (reset_count[-1] == 0)
    fresh_state = jnp.einsum(
        "sn,shp->hnp",
        write_part,
        feature_part * tail_weight.T[:, :, None],
        precision=lax.Precision.HIGHEST,
    )
    return (block_decay[:, None, None] * carry_state + fresh_state, result)


def link_states(earlier, later):
    return (earlier[0] * later[0], later[0][:, None, None] * earlier[1] + later[1])


def shards(mixer_input, write_rows, read_rows, log_decay, skip_gain, reset_offsets, grad_out):
    write_whole, read_whole = (
        lax.all_gather(write_rows, "head", axis=0, tiled=True),
        lax.all_gather(read_rows, "head", axis=0, tiled=True),
    )
    token_count = mixer_input.shape[0]
    head_count = log_decay.shape[0]
    head_width = mixer_input.shape[1] // head_count
    feature_full = mixer_input.astype(jnp.float32).reshape(token_count, head_count, head_width)
    write_full = write_whole.astype(jnp.float32)
    read_full = read_whole.astype(jnp.float32)
    cotangent = grad_out.astype(jnp.float32).reshape(token_count, head_count, head_width)
    positions = jnp.arange(token_count, dtype=jnp.int32)
    resets = jnp.any(positions[:, None] == reset_offsets[0][None, :], axis=1).astype(jnp.float32)
    cum_log = jnp.cumsum(log_decay, axis=1)
    reset_count = jnp.cumsum(resets)
    input_gain = jnp.sqrt(-jnp.expm1(2.0 * log_decay))
    tail_weight = (
        jnp.exp(cum_log[:, -1:] - cum_log) * (reset_count == reset_count[-1])[None, :] * input_gain
    )
    local_state = jnp.einsum(
        "tn,thp->hnp",
        write_full,
        feature_full * tail_weight.T[:, :, None],
        precision=lax.Precision.HIGHEST,
    )
    block_decay = jnp.exp(cum_log[:, -1]) * (reset_count[-1] == 0)
    entry_decay = jnp.exp(cum_log) * (reset_count == 0)[None, :]
    local_grad = jnp.einsum(
        "tn,thp->hnp",
        read_full,
        cotangent * entry_decay.T[:, :, None],
        precision=lax.Precision.HIGHEST,
    )
    identity = (jnp.ones_like(block_decay), jnp.zeros_like(local_state))
    decay_before, state_in = entering(
        (block_decay, local_state), "seq", link_states, identity, False
    )
    decay_after, grad_in = entering((block_decay, local_grad), "seq", link_states, identity, True)
    spans = token_count // SPAN
    log_blocks = log_decay.reshape(head_count, spans, SPAN).transpose(1, 0, 2)
    reset_blocks = resets.reshape(spans, SPAN)

    def block_forward(feature_arg, write_arg, read_arg):
        feature_blocks = feature_arg.reshape(spans, SPAN, head_count, head_width)
        write_blocks = write_arg.reshape(spans, SPAN, write_arg.shape[1])
        read_blocks = read_arg.reshape(spans, SPAN, read_arg.shape[1])

        def advance(carry_state, inputs):
            return span_update(carry_state, inputs, skip_gain)

        end_state, outputs = lax.scan(
            advance, state_in, (feature_blocks, write_blocks, read_blocks, log_blocks, reset_blocks)
        )
        return (outputs.reshape(token_count, head_count, head_width), end_state)

    outputs, pullback = jax.vjp(block_forward, feature_full, write_full, read_full)
    grad_feature, grad_write_all, grad_read_all = pullback((cotangent, grad_in))
    grad_write, grad_read = (
        lax.psum_scatter(grad_write_all, "head", scatter_dimension=0, tiled=True),
        lax.psum_scatter(grad_read_all, "head", scatter_dimension=0, tiled=True),
    )
    grad_input = grad_feature.reshape(token_count, head_count * head_width).astype(jnp.bfloat16)
    return (grad_input, grad_write, grad_read)


def solution(mesh):
    in_specs = (
        P("seq", "head"),
        P(("seq", "head"), None),
        P(("seq", "head"), None),
        P("head", "seq"),
        P("head"),
        P("seq", None),
        P("seq", "head"),
    )
    out_specs = (P("seq", "head"), P(("seq", "head"), None), P(("seq", "head"), None))
    return jax.shard_map(shards, mesh=mesh, in_specs=in_specs, out_specs=out_specs, check_vma=False)
```

profile of v0, /device:TPU:4, one launch (start us, length us, event | category | flops | bytes accessed | tf_op | source)
XLA Modules:
  0.0 574.7 jit_solution(11024643300926106177)
XLA Ops:
  18.5 13.6 %all_gather.28 = bf16[2048,128]{1,0:T(8,128)(2,1)S(1)} all-gather(bf16[256,128]{1,0:T(8,128)(2,1)S(1)} %copy-done.5), channel_id=1, replica_groups=mesh['seq'=32,'head'=8] {'head'}, dimensions={0}, use_global_device_ids=true | all-gather | bytes 589824 | tf_op jit(solution)/shard_map/all_gather | solution.py:62
  40.3 13.2 %all_gather.25 = bf16[2048,128]{1,0:T(8,128)(2,1)S(1)} all-gather(bf16[256,128]{1,0:T(8,128)(2,1)S(1)} %copy-done.6), channel_id=1, replica_groups=mesh['seq'=32,'head'=8] {'head'}, dimensions={0}, use_global_device_ids=true | all-gather | bytes 589824 | tf_op jit(solution)/shard_map/all_gather | solution.py:63
  60.3 74.4 %all-reduce = f32[320]{0:T(512)S(1)} all-reduce(f32[320]{0:T(512)S(1)} %dynamic-update-slice), channel_id=2, replica_groups=mesh['seq'=32,'head'=8] {'seq'}, use_global_device_ids=true, to_apply=%add | all-reduce | flops 320 | bytes 2560
  134.8 5.0 copy.94
  144.9 7.4 %copy.95 = f32[80,8,8,256]{3,2,1,0:T(8,128)} copy(f32[80,8,8,256]{3,1,2,0:T(8,128)} %bitcast.375) | data formatting | bytes 10485760
  155.5 115.7 %while.83 = (s32[]{:T(128)}, f32[10,128,64]{1,2,0:T(8,128)S(1)}, f32[8,128,256]{1,2,0:T(8,128)}, f32[8,10,256,256]{3,2,1,0:T(8,128)}, f32[8,10,1,256]{3,1,2,0:T(...) while((s32[]{:T(128)}, f32[10,128,64]{1,2,0:T(8,128)S(1)}, ...), condition=%wide.region_14.15_spmd.clone.clone, body=%wide.region_9.14_spmd.clone.sunk.clone | while | flops 356031040 | bytes 10219655 | solution.py:111
  271.2 42.5 %while.80 = (s32[]{:T(128)}, f32[10,128,64]{2,1,0:T(8,128)S(1)}, s32[]{:T(128)}, f32[32,10]{1,0:T(8,128)S(1)}, f32[32,10,128,64]{2,3,1,0:T(8,128)}) while((s32[]{:T(128)}, f32[10,128,64]{2,1,0:T(8,128)S(1)}, s32[]{:T(128)}, f32[32,10]{1,0:T(8,128)S(1)}, f32[32,10,128,64]{2,3,1,0:T(8,128)}) %tuple.184), condition=%wide.region_6.7_spmd.clone, body=%wide.region_5.6_spmd.sunk.clone | while | flops 163846 | bytes 2293995 | solution.py:22
  315.1 182.8 %while.82 = (s32[]{:T(128)}, f32[10,128,64]{1,2,0:T(8,128)S(1)}, bf16[8,256,10,64]{1,3,2,0:T(8,128)(2,1)}, f32[8,256,128]{2,1,0:T(8,128)S(1)}, f32[8,256,128]{2,...) while((s32[]{:T(128)}, f32[10,128,64]{1,2,0:T(8,128)S(1)}, ...), condition=%wide.region_17.18_spmd.clone, body=%wide.region_15.17_spmd.sunk.clone | while | flops 2217705472 | bytes 16956240 | solution.py:111
  319.6 4.2 fusion.184
  323.8 4.4 fusion.185
  346.7 4.4 fusion.185
  365.3 4.2 fusion.184
  369.5 4.4 fusion.185
  392.3 4.4 fusion.185
  411.0 4.2 fusion.184
  415.2 4.4 fusion.185
  433.8 4.2 fusion.184
  438.0 4.4 fusion.185
  456.7 4.2 fusion.184
  460.9 4.4 fusion.185
  479.5 4.2 fusion.184
  483.8 4.4 fusion.185
  506.3 25.5 %reduce-scatter.3.cloned.1.call-done = f32[256,128]{1,0:T(8,128)} async-done(((f32[2048,128]{1,0:T(8,128)}), f32[256,128]{1,0:T(8,128)}) %reduce-scatter.3.cloned.1.call-update) | async-done | bytes 131088 | tf_op jit(solution)/shard_map/reduce_scatter | solution.py:119
  531.9 36.3 %reduce-scatter.5.cloned.1.call-done = f32[256,128]{1,0:T(8,128)} async-done(((f32[2048,128]{1,0:T(8,128)}), f32[256,128]{1,0:T(8,128)}) %reduce-scatter.5.cloned.1.call-update) | async-done | bytes 131088 | tf_op jit(solution)/shard_map/reduce_scatter | solution.py:120
  (545 shorter events, 317.8 us)
Async XLA Ops:
  7.2 145.1 %all-gather.8.cloned.1.call-start = ((), (), s32[]{:S(2)}) async-start(), calls=%async_computation.5 | async-start | bytes 10813440 | tf_op jit(solution)/shard_map/all_gather | solution.py:13
  14.8 3.7 copy-start.5
  17.8 14.5 %copy-start.3 = (f32[10,2048]{1,0:T(8,128)S(1)}, f32[10,2048]{1,0:T(8,128)}, u32[]{:S(2)}) copy-start(f32[10,2048]{1,0:T(8,128)} %param.18) | copy-start | bytes 245764
  18.5 14.6 %copy-start = (f32[2048,640]{0,1:T(8,128)}, f32[2048,640]{0,1:T(8,128)S(1)}, u32[]{:S(2)}) copy-start(f32[2048,640]{0,1:T(8,128)S(1)} %convert_element_type.76) | copy-start | bytes 15728644
  36.5 3.8 copy-start.6
  36.5 234.6 %all-gather.6.cloned.1.call-start = ((), (), s32[]{:S(2)}) async-start(), calls=%async_computation.4 | async-start | bytes 10813440 | tf_op jit(solution)/shard_map/all_gather | solution.py:13
  39.5 14.0 %copy-start.4 = (f32[2048,10]{0,1:T(8,128)S(1)}, f32[2048,10]{0,1:T(8,128)}, u32[]{:S(2)}) copy-start(f32[2048,10]{0,1:T(8,128)} %get-tuple-element.1043) | copy-start | bytes 245764
  40.2 13.3 %copy-start.1 = (f32[2048,640]{0,1:T(8,128)}, f32[2048,640]{0,1:T(8,128)S(1)}, u32[]{:S(2)}) copy-start(f32[2048,640]{0,1:T(8,128)S(1)} %convert_element_type.74) | copy-start | bytes 15728644
  40.2 18.5 %copy-start.8 = (u32[256]{0:T(256)S(1)}, u32[256]{0:T(256)}, u32[]{:S(2)}) copy-start(u32[256]{0:T(256)} %constant.201) | copy-start | bytes 3076
  56.8 475.0 %reduce-scatter.3.cloned.1.call-start = ((), (), s32[]{:S(2)}) async-start(), calls=%async_computation.2 | async-start | bytes 1179648 | tf_op jit(solution)/shard_map/reduce_scatter | solution.py:119
  271.2 43.9 %copy-start.7 = (f32[10]{0:T(128)S(1)}, f32[10]{0:T(128)}, u32[]{:S(2)}) copy-start(f32[10]{0:T(128)} %param.19) | copy-start | bytes 124
  497.9 1.0 copy-start.2
  498.9 69.3 %reduce-scatter.5.cloned.1.call-start = ((), (), s32[]{:S(2)}) async-start(), calls=%async_computation.3 | async-start | bytes 1179648 | tf_op jit(solution)/shard_map/reduce_scatter | solution.py:120
Sparse Core Ops, SparseCore 0:
  36.6 110.4 all-gather.7
  149.7 105.9 all-gather.5
  499.0 32.8 reduce-scatter.2
  534.8 33.3 reduce-scatter.4
where the time goes:
time: 579 us; the launch traced here: 575 us
  matrix products  184 us (32%)
  local copies, waits for them, and re-layouts  124 us (21%)
  blocking collectives  101 us (17%)
  other arithmetic  78.9 us (14%)
  waiting for transfers between devices  62.2 us (11%)
  between operations  15.4 us (3%)
  loops' own time  8.71 us (2%)
    unnamed x1, blocking collectives  74.4 us
    dot_general x16, matrix products, span_update(): jnp.einsum('hts,shp->thp', weights, feature_part, precision=lax.Precision...  68.6 us
    dynamic_update_slice x32, other arithmetic, block_forward(): lax.scan(advance, state_in, (feature_blocks, write_blocks, read_blocks, l...  45.9 us
    dot_general x24, matrix products, span_update(): jnp.einsum('sn,shp->hnp', write_part, feature_part * tail_weight.T[:, :,...  39.4 us
    dynamic_slice x62, local copies, waits for them, and re-layouts, one(): lax.dynamic_index_in_dim(a, source, 0, False)  38.2 us
    dot_general x24, matrix products, span_update(): scores = jnp.dot(read_part, write_part.T, precision=lax.Precision.HIGHEST)  37.9 us
    reduce_scatter x1, waiting for transfers between devices, shards(): lax.psum_scatter(grad_read_all, 'head', scatter_dimension=0, tiled=True)  36.3 us
    dot_general x16, matrix products, span_update(): jnp.einsum('tn,hnp->thp', read_part, carry_state, precision=lax.Precision...  31.6 us
  transfers between devices with their start and end apart: 4, of which 2 were waited for; matrix products, arithmetic and copies ran while one was open for 25% of the time, Pallas kernels for 0%

commit v1 on v0

--- a/solution.py
+++ b/solution.py
@@ -4,6 +4,27 @@
 from jax.sharding import PartitionSpec as P
 
 SPAN = 256
+
+
+def gather_around(value, axis, dim):
+    size, position, rows = (lax.axis_size(axis), lax.axis_index(axis), value.shape[dim])
+    right = [(i, (i + 1) % size) for i in range(size)]
+    downward = [(i, (i - 1) % size) for i in range(size)]
+    out = jnp.zeros((*value.shape[:dim], size * rows, *value.shape[dim + 1 :]), value.dtype)
+    out = lax.dynamic_update_slice_in_dim(out, value, position * rows, axis=dim)
+    from_left = from_right = value
+    middle = size // 2
+    for lap in range(1, middle + 1):
+        from_left = lax.ppermute(from_left, axis, right)
+        out = lax.dynamic_update_slice_in_dim(
+            out, from_left, (position - lap) % size * rows, axis=dim
+        )
+        if lap < size - middle:
+            from_right = lax.ppermute(from_right, axis, downward)
+            out = lax.dynamic_update_slice_in_dim(
+                out, from_right, (position + lap) % size * rows, axis=dim
+            )
+    return out
 
 
 def entering(part, axis, combine, identity, reverse):
@@ -60,7 +81,7 @@
 def shards(mixer_input, write_rows, read_rows, log_decay, skip_gain, reset_offsets, grad_out):
     write_whole, read_whole = (
         lax.all_gather(write_rows, "head", axis=0, tiled=True),
-        lax.all_gather(read_rows, "head", axis=0, tiled=True),
+        gather_around(read_rows, "head", 0),
     )
     token_count = mixer_input.shape[0]
     head_count = log_decay.shape[0]

time: 579 us -> 588 us (1.016)
  blocking collectives: 101 us -> 87.9 us
  starting transfers between devices: 0.43 us -> 9.5 us
  waiting for transfers between devices: 62.2 us -> 68.8 us
  local copies, waits for them, and re-layouts: 124 us -> 130 us
    all_gather x1 -> x0, blocking collectives: 13.2 us -> none  [shards(): lax.all_gather(read_rows, 'head', axis=0, tiled=True)]
    ppermute x0 -> x7, starting transfers between devices: none -> 9.07 us  [the longest x3 8.69 us: gather_around(): from_right = lax.ppermute(from_right, axis, downward)]
    ppermute x0 -> x7, waiting for transfers between devices: none -> 8.5 us  [the longest x4 8.35 us: gather_around(): from_left = lax.ppermute(from_left, axis, right)]
    unnamed x33 -> x35, local copies, waits for them, and re-layouts: 28.9 us -> 30.2 us
  transfers between devices with their start and end apart: 4 -> 11, of which waited for: 2 -> 6; matrix products, arithmetic and copies ran while one was open for 25% -> 26% of each run, Pallas kernels for 0% -> 0%
where the time goes in v1:
time: 588 us; the launch traced here: 582 us
  matrix products  179 us (30%)
  local copies, waits for them, and re-layouts  130 us (22%)
  blocking collectives  87.9 us (15%)
  other arithmetic  84.2 us (14%)
  waiting for transfers between devices  68.8 us (12%)
  between operations  15.5 us (3%)
  starting transfers between devices  9.5 us (2%)
  loops' own time  8.07 us (1%)
    unnamed x1, blocking collectives  74.1 us
    dot_general x16, matrix products, span_update(): jnp.einsum('hts,shp->thp', weights, feature_part, precision=lax.Precision...  68.6 us
    dynamic_update_slice x32, other arithmetic, block_forward(): lax.scan(advance, state_in, (feature_blocks, write_blocks, read_blocks, l...  50.8 us
    dot_general x24, matrix products, span_update(): jnp.einsum('sn,shp->hnp', write_part, feature_part * tail_weight.T[:, :,...  39.5 us
    dynamic_slice x62, local copies, waits for them, and re-layouts, one(): lax.dynamic_index_in_dim(a, source, 0, False)  38.2 us
    reduce_scatter x1, waiting for transfers between devices, shards(): lax.psum_scatter(grad_read_all, 'head', scatter_dimension=0, tiled=True)  36.3 us
    dot_general x24, matrix products, span_update(): scores = jnp.dot(read_part, write_part.T, precision=lax.Precision.HIGHEST)  32.6 us
    dot_general x16, matrix products, span_update(): jnp.einsum('tn,hnp->thp', read_part, carry_state, precision=lax.Precision...  31.6 us
  transfers between devices with their start and end apart: 11, of which 6 were waited for; matrix products, arithmetic and copies ran while one was open for 26% of the time, Pallas kernels for 0%

profile of v1, /device:TPU:4, one launch (start us, length us, event | category | flops | bytes accessed | tf_op | source)
XLA Modules:
  0.0 582.4 jit_solution(5943541975965832612)
XLA Ops:
  18.6 13.8 %all_gather.24 = bf16[2048,128]{1,0:T(8,128)(2,1)S(1)} all-gather(bf16[256,128]{1,0:T(8,128)(2,1)S(1)} %copy-done.6), channel_id=1, replica_groups=mesh['seq'=32,'head'=8] {'head'}, dimensions={0}, use_global_device_ids=true | all-gather | bytes 589824 | tf_op jit(solution)/shard_map/all_gather | solution.py:83
  40.6 74.1 %all-reduce = f32[320]{0:T(512)S(1)} all-reduce(f32[320]{0:T(512)S(1)} %dynamic-update-slice), channel_id=2, replica_groups=mesh['seq'=32,'head'=8] {'seq'}, use_global_device_ids=true, to_apply=%add | all-reduce | flops 320 | bytes 2560
  114.8 5.1 copy.94
  123.9 4.4 copy.72
  133.2 4.9 copy.95
  150.0 4.7 collective-permute-done.6
  162.6 118.5 %while.83 = (s32[]{:T(128)}, f32[10,128,64]{1,2,0:T(8,128)S(1)}, f32[8,128,256]{1,2,0:T(8,128)}, f32[8,10,256,256]{3,2,1,0:T(8,128)}, f32[8,10,1,256]{3,1,2,0:T(...) while((s32[]{:T(128)}, f32[10,128,64]{1,2,0:T(8,128)S(1)}, ...), condition=%wide.region_14.15_spmd.clone.clone, body=%wide.region_9.14_spmd.clone.sunk.clone | while | flops 356031040 | bytes 10220163 | solution.py:132
  281.2 42.3 %while.80 = (s32[]{:T(128)}, f32[10,128,64]{2,1,0:T(8,128)S(1)}, s32[]{:T(128)}, f32[32,10]{1,0:T(8,128)S(1)}, f32[32,10,128,64]{2,3,1,0:T(8,128)}) while((s32[]{:T(128)}, f32[10,128,64]{2,1,0:T(8,128)S(1)}, s32[]{:T(128)}, f32[32,10]{1,0:T(8,128)S(1)}, f32[32,10,128,64]{2,3,1,0:T(8,128)}) %tuple.184), condition=%wide.region_6.7_spmd.clone, body=%wide.region_5.6_spmd.sunk.clone | while | flops 163846 | bytes 2293995 | solution.py:43
  323.9 183.6 %while.82 = (s32[]{:T(128)}, f32[10,128,64]{1,2,0:T(8,128)S(1)}, bf16[8,256,10,64]{1,3,2,0:T(8,128)(2,1)}, f32[8,256,128]{2,1,0:T(8,128)S(1)}, f32[8,256,128]{2,...) while((s32[]{:T(128)}, f32[10,128,64]{1,2,0:T(8,128)S(1)}, ...), condition=%wide.region_17.18_spmd.clone, body=%wide.region_15.17_spmd.sunk.clone | while | flops 2217705472 | bytes 16956240 | solution.py:132
  333.3 4.4 fusion.185
  356.3 4.4 fusion.185
  379.2 4.4 fusion.185
  397.2 4.2 fusion.184
  402.1 4.4 fusion.185
  420.2 4.2 fusion.184
  425.1 4.4 fusion.185
  443.1 4.2 fusion.184
  448.0 4.4 fusion.185
  466.1 4.2 fusion.184
  471.0 4.4 fusion.185
  489.0 4.2 fusion.184
  493.9 4.4 fusion.185
  515.9 23.7 %reduce-scatter.3.cloned.1.call-done = f32[256,128]{1,0:T(8,128)} async-done(((f32[2048,128]{1,0:T(8,128)}), f32[256,128]{1,0:T(8,128)}) %reduce-scatter.3.cloned.1.call-update) | async-done | bytes 131088 | tf_op jit(solution)/shard_map/reduce_scatter | solution.py:140
  539.6 36.3 %reduce-scatter.5.cloned.1.call-done = f32[256,128]{1,0:T(8,128)} async-done(((f32[2048,128]{1,0:T(8,128)}), f32[256,128]{1,0:T(8,128)}) %reduce-scatter.5.cloned.1.call-update) | async-done | bytes 131088 | tf_op jit(solution)/shard_map/reduce_scatter | solution.py:141
  (569 shorter events, 339.0 us)
Async XLA Ops:
  7.2 152.0 %all-gather.8.cloned.1.call-start = ((), (), s32[]{:S(2)}) async-start(), calls=%async_computation.5 | async-start | bytes 10813440 | tf_op jit(solution)/shard_map/all_gather | solution.py:34
  14.8 3.7 copy-start.6
  17.8 14.7 %copy-start.5 = (f32[10,2048]{1,0:T(8,128)S(1)}, f32[10,2048]{1,0:T(8,128)}, u32[]{:S(2)}) copy-start(f32[10,2048]{1,0:T(8,128)} %param.18) | copy-start | bytes 245764
  18.5 14.1 %copy-start = (f32[2048,640]{0,1:T(8,128)}, f32[2048,640]{0,1:T(8,128)S(1)}, u32[]{:S(2)}) copy-start(f32[2048,640]{0,1:T(8,128)S(1)} %convert_element_type.76) | copy-start | bytes 15728644
  18.5 17.5 %copy-start.7 = (bf16[256,128]{1,0:T(8,128)(2,1)S(1)}, bf16[256,128]{1,0:T(8,128)(2,1)}, u32[]{:S(2)}) copy-start(bf16[256,128]{1,0:T(8,128)(2,1)} %param.17) | copy-start | bytes 196612
  18.5 20.5 %copy-start.9 = (u32[256]{0:T(256)S(1)}, u32[256]{0:T(256)}, u32[]{:S(2)}) copy-start(u32[256]{0:T(256)} %constant.261) | copy-start | bytes 3076
  36.0 245.1 %all-gather.6.cloned.1.call-start = ((), (), s32[]{:S(2)}) async-start(), calls=%async_computation.4 | async-start | bytes 10813440 | tf_op jit(solution)/shard_map/all_gather | solution.py:34
  36.1 103.9 %collective-permute-start = (bf16[256,128]{1,0:T(8,128)(2,1)S(1)}, bf16[256,128]{1,0:T(8,128)(2,1)S(1)}, u32[]{:S(2)}, u32[]{:S(2)}) collective-permute-start(bf16[256,128]{1,0:T(8,128)(2,1)S(1)} %copy-done.7), channel_id=1, source_target_pairs={{0,1},{1,2},{2,3},{3,4},{4,5},{5,6},{6,7},{7,0},{8,9},{9,10},{10,1... | collective-permute-start | bytes 196616 | tf_op jit(solution)/shard_map/ppermute | solution.py:18
  36.4 103.6 %collective-permute-start.1 = (bf16[256,128]{1,0:T(8,128)(2,1)S(1)}, bf16[256,128]{1,0:T(8,128)(2,1)S(1)}, u32[]{:S(2)}, u32[]{:S(2)}) collective-permute-start(bf16[256,128]{1,0:T(8,128)(2,1)S(1)} %copy-done.7), channel_id=1, source_target_pairs={{0,7},{1,0},{2,1},{3,2},{4,3},{5,4},{6,5},{7,6},{8,15},{9,8},{10,9... | collective-permute-start | bytes 196616 | tf_op jit(solution)/shard_map/ppermute | solution.py:23
  130.8 2.4 copy-start.1
  138.0 17.7 %copy-start.2 = (f32[2048,640]{0,1:T(8,128)S(1)}, f32[2048,640]{0,1:T(8,128)}, u32[]{:S(2)}) copy-start(f32[2048,640]{0,1:T(8,128)} %copy-done.1) | copy-start | bytes 15728644
  140.0 4.9 collective-permute-start.2
  140.0 4.9 collective-permute-start.3
  144.9 4.9 collective-permute-start.4
  144.9 5.1 collective-permute-start.5
  149.8 4.9 collective-permute-start.6
  159.1 380.4 %reduce-scatter.3.cloned.1.call-start = ((), (), s32[]{:S(2)}) async-start(), calls=%async_computation.2 | async-start | bytes 1179648 | tf_op jit(solution)/shard_map/reduce_scatter | solution.py:140
  281.2 42.7 %copy-start.8 = (f32[10]{0:T(128)S(1)}, f32[10]{0:T(128)}, u32[]{:S(2)}) copy-start(f32[10]{0:T(128)} %param.19) | copy-start | bytes 124
  507.4 1.0 copy-start.3
  507.5 1.3 copy-start.4
  508.5 67.4 %reduce-scatter.5.cloned.1.call-start = ((), (), s32[]{:S(2)}) async-start(), calls=%async_computation.3 | async-start | bytes 1179648 | tf_op jit(solution)/shard_map/reduce_scatter | solution.py:141
Sparse Core Ops, SparseCore 0:
  36.1 110.0 all-gather.7
  159.2 103.9 all-gather.5
  508.6 30.9 reduce-scatter.2
  542.5 33.3 reduce-scatter.4
